TPU v7x, 32 devices: a whole 2x2x4 slice. The times are simulated.
32 devices in a mesh: parts: 2 (over y), vocab: 4 (over z), docs: 4 (over x, core).
Axes of the slice: x: 2, y: 2, z: 4, core: 2. Of those that a mesh axis runs over, the one named last changes fastest.
Arguments:
- lambda_topics: float32 [2048, 4096], P('docs', 'vocab'), may hold values from 0.025 to 120, as said below
- gamma_start: float32 [2048, 2048], P(('parts', 'docs')), parts along dimension 0, may hold values from 0.5 to 2
- tile_counts: int32 [8, 4, 16, 128, 128], P(('parts', 'docs'), 'vocab'), parts along dimension 0, may hold values from 0 to 12, as said below
- tile_place: int32 [8, 4, 16, 2], P(('parts', 'docs'), 'vocab'), parts along dimension 0, may hold values from 0 to 7, as said below
- tile_live: int32 [8, 4], P(('parts', 'docs'), 'vocab'), parts along dimension 0, may hold values from 1 to 16, as said below
Outputs:
- gamma: float32 [2048, 2048], P(('parts', 'docs', 'vocab')), parts along dimension 0
- lambda_new: float32 [4096, 4096], P(('parts', 'docs'), 'vocab'), parts along dimension 0
There are 2 independent parts, one for each index of `parts`. A program takes and returns all parts, laid end to end along the dimension named above; an argument that names none is the same for every part. Nothing has to cross between parts.
Inputs may be any that keep to these rules, and one draw needn't show every extreme that they name: `lambda_topics`: Positive. `tile_counts`: slots at or past the group's and shard's live count hold only zeros. `tile_place`: the 16 slots of each group and shard name every pair of doc block and word block of that group's documents and that shard's words once. `tile_live`: some group and shard has all 16 slots live.
All inputs are finite; a program needn't handle non-finite values.
Results may differ from a plain program's by a relative error of at most 0.02.
Values may be sent and summed in bfloat16 or wider, within the bound.
A program may use at most 128 MiB of HBM per device.

v0:
```python
import jax
import jax.numpy as jnp
from jax import lax
from jax.sharding import PartitionSpec as P

TILE = 128
ITERS = 3


alpha_prior = 0.05
eta_prior = 0.01
step_weight = 0.5
corpus_scale = 4.0


def expected_theta(gamma):
    spread = lax.digamma(gamma) - lax.digamma(jnp.sum(gamma, 1, keepdims=True))
    return jnp.exp(spread).astype(jnp.bfloat16)


def tile_pass(exp_theta, exp_beta, counts, place, live, with_sums):

    def tile_one_tile(position, carry):
        ratios, total = carry
        row_start = place[position, 0] * TILE
        col_start = place[position, 1] * TILE
        theta_block = lax.dynamic_slice_in_dim(exp_theta, row_start, TILE, 0)
        beta_block = lax.dynamic_slice_in_dim(exp_beta, col_start, TILE, 1)
        norm = jnp.dot(theta_block, beta_block, preferred_element_type=jnp.float32)
        weights = lax.dynamic_index_in_dim(counts, position, 0, keepdims=False).astype(jnp.float32)
        ratio = (weights / norm).astype(jnp.bfloat16)
        ratios = lax.dynamic_update_index_in_dim(ratios, ratio, position, 0)
        if with_sums:
            part = lax.dot_general(
                ratio, beta_block, (((1,), (1,)), ((), ())), preferred_element_type=jnp.float32
            )
            current = lax.dynamic_slice_in_dim(total, row_start, TILE, 0)
            total = lax.dynamic_update_slice_in_dim(total, current + part, row_start, 0)
        return (ratios, total)

    ratios = jnp.zeros(counts.shape, jnp.bfloat16)
    total = jnp.zeros((exp_theta.shape[0], exp_theta.shape[1]), jnp.float32)
    return lax.fori_loop(0, live, tile_one_tile, (ratios, total))


def on_device(lambda_topics, gamma_start, tile_counts, tile_place, tile_live):
    counts = tile_counts[0, 0]
    place = tile_place[0, 0]
    live = tile_live[0, 0]
    share_rows = lambda_topics.shape[0]
    rowsum = lax.psum(jnp.sum(lambda_topics, 1), "vocab")
    share_beta = jnp.exp(lax.digamma(lambda_topics) - lax.digamma(rowsum)[:, None]).astype(
        jnp.bfloat16
    )
    exp_beta = lax.all_gather(share_beta, "docs", axis=0, tiled=True)
    own_rows = gamma_start.shape[0] // lax.axis_size("vocab")
    own_start = lax.axis_index("vocab") * own_rows
    exp_theta = expected_theta(gamma_start)
    gamma_rows = lax.dynamic_slice_in_dim(gamma_start, own_start, own_rows, 0)
    for step in range(ITERS):
        ratios, partial_value = tile_pass(exp_theta, exp_beta, counts, place, live, True)
        total = lax.psum(partial_value.astype(jnp.bfloat16), "vocab").astype(jnp.float32)
        gamma_full = alpha_prior + exp_theta.astype(jnp.float32) * total
        exp_theta = expected_theta(gamma_full)
        gamma_rows = lax.dynamic_slice_in_dim(gamma_full, own_start, own_rows, 0)
    ratios, unused = tile_pass(exp_theta, exp_beta, counts, place, live, False)
    words = exp_beta.shape[1]
    theta_cols = exp_theta

    def word_one_tile(position, acc):
        row_start = place[position, 0] * TILE
        col_start = place[position, 1] * TILE
        theta_block = lax.dynamic_slice_in_dim(theta_cols, row_start, TILE, 0)
        ratio = lax.dynamic_index_in_dim(ratios, position, 0, keepdims=False)
        part = lax.dot_general(
            theta_block, ratio, (((0,), (0,)), ((), ())), preferred_element_type=jnp.float32
        )
        current = lax.dynamic_slice_in_dim(acc, col_start, TILE, 1)
        return lax.dynamic_update_slice_in_dim(acc, current + part, col_start, 1)

    sstats = lax.psum_scatter(
        lax.fori_loop(
            0,
            live,
            word_one_tile,
            jnp.zeros((lax.axis_size("docs") * share_rows, words), jnp.float32),
        ).astype(jnp.bfloat16),
        "docs",
        scatter_dimension=0,
        tiled=True,
    ).astype(jnp.float32)
    lambda_new = (1.0 - step_weight) * lambda_topics + step_weight * (
        eta_prior + corpus_scale * share_beta.astype(jnp.float32) * sstats
    )
    return (gamma_rows, lambda_new)


def solution(mesh):
    return jax.shard_map(
        on_device,
        mesh=mesh,
        in_specs=(
            P("docs", "vocab"),
            P(("parts", "docs"), None),
            P(("parts", "docs"), "vocab", None, None, None),
            P(("parts", "docs"), "vocab", None, None),
            P(("parts", "docs"), "vocab"),
        ),
        out_specs=(P(("parts", "docs", "vocab"), None), P(("parts", "docs"), "vocab")),
        check_vma=False,
    )
```

profile of v0, /device:TPU:11, one launch (start us, length us, event | category | flops | bytes accessed | tf_op | source)
XLA Modules:
  0.0 743.4 jit_solution(3671109214002335278)
XLA Ops:
  7.2 1.9 reduce_sum.46
  9.1 7.3 psum.28
  16.5 15.5 %fusion.53 = bf16[512,1024]{1,0:T(8,128)(2,1)} fusion(f32[512,1024]{1,0:T(8,128)S(1)} %copy-done.1, f32[512]{0:T(512)S(1)} %select_select_fusion), kind=kLoop, calls=%fused_computation.72 | loop fusion | flops 40370176 | bytes 3147776 | tf_op jit(solution)/shard_map/convert_element_type | solution.py:52
  32.0 1.9 reduce_sum.45
  34.2 14.6 %fusion.48 = bf16[256,2048]{1,0:T(8,128)(2,1)S(1)} fusion(f32[256,2048]{1,0:T(8,128)S(1)} %copy-done.4, f32[256]{0:T(256)S(1)} %compare_select_fusion.3), kind=kLoop, calls=%fused_computation.67 | loop fusion | flops 40370176 | bytes 3146752 | tf_op jit(solution)/shard_map/convert_element_type | solution.py:18
  48.8 20.2 %all-gather.2.cloned.1.call-done = bf16[2048,1024]{1,0:T(8,128)(2,1)} async-done(((bf16[512,1024]{1,0:T(8,128)(2,1)}), bf16[2048,1024]{1,0:T(8,128)(2,1)}) %all-gather.2.cloned.1.call-update) | async-done | bytes 4194320 | tf_op jit(solution)/shard_map/all_gather | solution.py:55
  69.2 70.8 %while.56 = (s32[]{:T(128)}, f32[256,2048]{1,0:T(8,128)S(1)}, s32[]{:T(128)}, s32[16,2]{0,1:T(2,128)S(1)}, s32[16,128,128]{2,1,0:T(8,128)}, /*index=5*/bf16[256,...) while((s32[]{:T(128)}, f32[256,2048]{1,0:T(8,128)S(1)}, ...), condition=%wide.region_4.5_spmd, body=%wide.region_3.4_spmd.sunk | while | flops 134529040 | bytes 3738391 | solution.py:43
  71.8 1.9 fusion.103
  98.2 1.9 fusion.103
  120.1 1.9 fusion.103
  141.4 51.8 %all-reduce.4.cloned.1.call-done = bf16[256,2048]{1,0:T(8,128)(2,1)} async-done(((bf16[256,2048]{1,0:T(8,128)(2,1)}), bf16[256,2048]{1,0:T(8,128)(2,1)}) %all-reduce.4.cloned.1.call-update) | async-done | bytes 1048592 | tf_op jit(solution)/shard_map/psum | solution.py:62
  193.2 16.2 %add_reduce_fusion.1 = f32[256]{0:T(256)S(1)} fusion(bf16[256,2048]{1,0:T(8,128)(2,1)} %all-reduce.4.cloned.1.call-done, f32[256]{0:T(256)S(1)} %compare_select_fusion.3, f32[256,2048]{1,0:T(8,128)} %param.16), kind=kLoop, calls=%fused_computation.96 | loop fusion | flops 42991360 | bytes 3147776 | tf_op jit(solution)/shard_map/reduce_sum | solution.py:17
  209.5 30.2 %fusion.58 = bf16[256,2048]{1,0:T(8,128)(2,1)S(1)} fusion(bf16[256,2048]{1,0:T(8,128)(2,1)S(1)} %copy-done.8, f32[256]{0:T(256)S(1)} %compare_select_fusion.2, f32[256]{0:T(256)S(1)} %compare_select_fusion.3, f32[256,2048]{1,0:T(8,128)S(1)} %copy-done.5), kind=kLoop, calls=%fused_computation.77 | loop fusion | flops 82837504 | bytes 4196352 | tf_op jit(solution)/shard_map/convert_element_type | solution.py:18
  240.0 70.9 %while.57 = (s32[]{:T(128)}, f32[256,2048]{1,0:T(8,128)S(1)}, s32[]{:T(128)}, s32[16,2]{0,1:T(2,128)S(1)}, s32[16,128,128]{2,1,0:T(8,128)}, /*index=5*/bf16[256,...) while((s32[]{:T(128)}, f32[256,2048]{1,0:T(8,128)S(1)}, ...), condition=%wide.region_8.9_spmd, body=%wide.region_7.8_spmd.sunk | while | flops 134529040 | bytes 3738391 | solution.py:43
  242.5 1.9 fusion.107
  268.9 1.9 fusion.107
  312.2 50.3 %all-reduce.6.cloned.1.call-done = bf16[256,2048]{1,0:T(8,128)(2,1)} async-done(((bf16[256,2048]{1,0:T(8,128)(2,1)}), bf16[256,2048]{1,0:T(8,128)(2,1)}) %all-reduce.6.cloned.1.call-update) | async-done | bytes 1048592 | tf_op jit(solution)/shard_map/psum | solution.py:62
  364.3 15.9 %fusion.63 = bf16[256,2048]{1,0:T(8,128)(2,1)S(1)} fusion(bf16[256,2048]{1,0:T(8,128)(2,1)S(1)} %copy-done.6, bf16[256,2048]{1,0:T(8,128)(2,1)} %copy-done, f32[256]{0:T(256)S(1)} %compare_select_fusion.1), kind=kLoop, calls=%fused_computation.82 | loop fusion | flops 42467328 | bytes 3146752 | tf_op jit(solution)/shard_map/convert_element_type | solution.py:18
  380.4 71.0 %while.58 = (s32[]{:T(128)}, f32[256,2048]{1,0:T(8,128)S(1)}, s32[]{:T(128)}, s32[16,2]{0,1:T(2,128)S(1)}, s32[16,128,128]{2,1,0:T(8,128)}, /*index=5*/bf16[256,...) while((s32[]{:T(128)}, f32[256,2048]{1,0:T(8,128)S(1)}, ...), condition=%wide.region_12.13_spmd, body=%wide.region_11.12_spmd.sunk | while | flops 134529040 | bytes 3738391 | solution.py:43
  382.9 1.9 fusion.111
  387.4 1.9 fusion.111
  409.3 1.9 fusion.111
  431.2 1.9 fusion.111
  452.6 50.3 %all-reduce.8.cloned.1.call-done = bf16[256,2048]{1,0:T(8,128)(2,1)} async-done(((bf16[256,2048]{1,0:T(8,128)(2,1)}), bf16[256,2048]{1,0:T(8,128)(2,1)}) %all-reduce.8.cloned.1.call-update) | async-done | bytes 1048592 | tf_op jit(solution)/shard_map/psum | solution.py:62
  504.7 15.6 %fusion.68 = (bf16[256,2048]{1,0:T(8,128)(2,1)S(1)}, f32[256,2048]{1,0:T(8,128)}) fusion(bf16[256,2048]{1,0:T(8,128)(2,1)S(1)} %copy-done.3, bf16[256,2048]{1,0:T(8,128)(2,1)S(1)} %get-tuple-element.768, f32[256]{0:T(256)S(1)} %compare_select_fusion), kind=kLoop, calls=%fused_computation.87 | loop fusion | flops 42467328 | bytes 5243904 | tf_op jit(solution)/shard_map/convert_element_type | solution.py:18
  520.4 62.9 %while.59 = (s32[]{:T(128)}, bf16[16,128,128]{2,1,0:T(8,128)(2,1)S(1)}, s32[]{:T(128)}, s32[16,128,128]{2,1,0:T(8,128)}, s32[16,2]{0,1:T(2,128)S(1)}, /*index=5*...) while((s32[]{:T(128)}, ...), condition=%wide.region_16.17_spmd, body=%wide.region_15.16_spmd.sunk | while | flops 67158032 | bytes 1147171 | solution.py:43
  583.3 4.3 broadcast_in_dim.15
  587.6 83.9 %while.60 = (s32[]{:T(128)}, f32[2048,1024]{1,0:T(8,128)}, s32[]{:T(128)}, s32[16,2]{0,1:T(2,128)S(1)}, bf16[256,2048]{1,0:T(8,128)(2,1)S(1)}, /*index=5*/bf16[1...) while((s32[]{:T(128)}, f32[2048,1024]{1,0:T(8,128)}, ...), condition=%wide.region_18.19_spmd, body=%wide.region_17.18_spmd.sunk | while | flops 67371024 | bytes 2654491 | solution.py:82
  590.2 2.6 fusion.117
  595.4 2.6 fusion.117
  600.6 2.6 fusion.117
  605.7 2.6 fusion.117
  610.9 2.6 fusion.117
  616.1 2.7 fusion.117
  621.4 2.6 fusion.117
  626.5 2.6 fusion.117
  631.7 2.6 fusion.117
  636.9 2.6 fusion.117
  642.1 2.7 fusion.117
  647.4 2.6 fusion.117
  652.6 2.6 fusion.117
  657.8 2.6 fusion.117
  663.0 2.6 fusion.117
  668.2 2.6 fusion.117
  671.5 6.0 convert_element_type.108
  677.5 2.0 constant_dynamic-slice_fusion.10
  679.5 40.6 %reduce-scatter.2.cloned.1.call-done = bf16[512,1024]{1,0:T(8,128)(2,1)} async-done(((bf16[2048,1024]{1,0:T(8,128)(2,1)}), bf16[512,1024]{1,0:T(8,128)(2,1)}) %reduce-scatter.2.cloned.1.call-update) | async-done | bytes 1048592 | tf_op jit(solution)/shard_map/reduce_scatter | solution.py:81
  720.1 16.8 %add_multiply_fusion = f32[512,1024]{1,0:T(8,128)} fusion(f32[512,1024]{1,0:T(8,128)S(1)} %copy-done.2, bf16[512,1024]{1,0:T(8,128)(2,1)} %reduce-scatter.2.cloned.1.call-done, f32[512]{0:T(512)S(1)} %select_select_fusion), kind=kLoop, calls=%fused_computation.88 | loop fusion | flops 44040192 | bytes 5244928 | tf_op jit(solution)/shard_map/add | solution.py:92
  (177 shorter events, 151.2 us)
Async XLA Ops:
  7.2 9.3 %copy-start.1 = (f32[512,1024]{1,0:T(8,128)S(1)}, f32[512,1024]{1,0:T(8,128)}, u32[]{:S(2)}) copy-start(f32[512,1024]{1,0:T(8,128)} %param.15) | copy-start | bytes 6291460
  7.2 61.8 %all-gather.2.cloned.1.call-start = ((), (), s32[]{:S(2)}) async-start(), calls=%async_computation.1 | async-start | bytes 5242880 | tf_op jit(solution)/shard_map/all_gather | solution.py:55
  32.0 2.2 copy-start.4
  32.0 161.2 %all-reduce.4.cloned.1.call-start = ((), (), s32[]{:S(2)}) async-start(), calls=%async_computation.2 | async-start | bytes 2097152 | tf_op jit(solution)/shard_map/psum | solution.py:62
  34.2 35.0 %copy-start.7 = (s32[1,1,16,2]{2,3,1,0:T(2,128)S(1)}, s32[1,1,16,2]{2,3,1,0:T(2,128)}, u32[]{:S(2)}) copy-start(s32[1,1,16,2]{2,3,1,0:T(2,128)} %param.18) | copy-start | bytes 388
  141.2 68.3 %copy-start.5 = (f32[256,2048]{1,0:T(8,128)S(1)}, f32[256,2048]{1,0:T(8,128)}, u32[]{:S(2)}) copy-start(f32[256,2048]{1,0:T(8,128)} %param.16) | copy-start | bytes 6291460
  141.2 221.2 %all-reduce.6.cloned.1.call-start = ((), (), s32[]{:S(2)}) async-start(), calls=%async_computation.3 | async-start | bytes 2097152 | tf_op jit(solution)/shard_map/psum | solution.py:62
  193.2 16.3 %copy-start.8 = (bf16[256,2048]{1,0:T(8,128)(2,1)S(1)}, bf16[256,2048]{1,0:T(8,128)(2,1)}, u32[]{:S(2)}) copy-start(bf16[256,2048]{1,0:T(8,128)(2,1)} %all-reduce.4.cloned.1.call-done) | copy-start | bytes 3145732
  310.8 53.4 %copy-start = (bf16[256,2048]{1,0:T(8,128)(2,1)}, bf16[256,2048]{1,0:T(8,128)(2,1)S(1)}, u32[]{:S(2)}) copy-start(bf16[256,2048]{1,0:T(8,128)(2,1)S(1)} %get-tuple-element.771) | copy-start | bytes 3145732
  312.1 190.8 %all-reduce.8.cloned.1.call-start = ((), (), s32[]{:S(2)}) async-start(), calls=%async_computation.4 | async-start | bytes 2097152 | tf_op jit(solution)/shard_map/psum | solution.py:62
  362.5 1.8 copy-start.6
  452.6 267.5 %reduce-scatter.2.cloned.1.call-start = ((), (), s32[]{:S(2)}) async-start(), calls=%async_computation.5 | async-start | bytes 5242880 | tf_op jit(solution)/shard_map/reduce_scatter | solution.py:81
  502.9 1.8 copy-start.3
  677.5 42.6 %copy-start.2 = (f32[512,1024]{1,0:T(8,128)S(1)}, f32[512,1024]{1,0:T(8,128)}, u32[]{:S(2)}) copy-start(f32[512,1024]{1,0:T(8,128)} %param.15) | copy-start | bytes 6291460
Sparse Core Ops, SparseCore 0:
  32.1 36.8 all-gather.1
  141.3 51.8 all-reduce.3
  312.2 50.1 all-reduce.5
  452.7 50.1 all-reduce.7
  677.6 42.4 reduce-scatter.1
where the time goes:
time: 749 us; the launch traced here: 743 us
  waiting for transfers between devices  213 us (28%)
  loops' own time  158 us (21%)
  matrix products  151 us (20%)
  other arithmetic  142 us (19%)
  local copies, waits for them, and re-layouts  57.4 us (8%)
  between operations  14 us (2%)
    psum x3, waiting for transfers between devices, on_device(): lax.psum(partial_value.astype(jnp.bfloat16), 'vocab').astype(jnp.float32)  152 us
    another operation x4, loops' own time, tile_pass(): return lax.fori_loop(0, live, tile_one_tile, (ratios, total))  126 us
    dot_general x48, matrix products, tile_one_tile(): lax.dot_general(ratio, beta_block, (((1,), (1,)), ((), ())), preferred_el...  87.7 us
    convert_element_type x4, other arithmetic, expected_theta(): return jnp.exp(spread).astype(jnp.bfloat16)  76.3 us
    dot_general x16, matrix products, word_one_tile(): lax.dot_general(theta_block, ratio, (((0,), (0,)), ((), ())), preferred_e...  41.9 us
    reduce_scatter x1, waiting for transfers between devices, on_device(): lax.psum_scatter(lax.fori_loop(0, live, word_one_tile, jnp.zeros((lax.axi...  40.6 us
    another operation x1, loops' own time, on_device(): lax.fori_loop(0, live, word_one_tile, jnp.zeros((lax.axis_size('docs') *...  31.6 us
    dynamic_slice x48, local copies, waits for them, and re-layouts, tile_one_tile(): col_start = place[position, 1] * TILE  29.8 us
  transfers between devices with their start and end apart: 5, of which 5 were waited for; matrix products, arithmetic and copies ran while one was open for 3% of the time, Pallas kernels for 0%

commit v1 on v0

v1 whole, which is shorter than its diff:
```python
import jax
import jax.numpy as jnp
from jax import lax
from jax.sharding import PartitionSpec as P

alpha_prior = 0.05
eta_prior = 0.01
step_weight = 0.5
corpus_scale = 4.0


def exp_digamma(x, offset):
    y = x + 4.0
    a = x * (x + 3.0)
    p = a * (a + 2.0)
    r = 1.0 / (p * y)
    q = p * r
    s = q * q
    shift = (2.0 * x + 3.0) * (2.0 * a + 2.0) * (y * r)
    tail = q * 0.5 + s * (1.0 / 12 - s * (1.0 / 120 - s * (1.0 / 252 - s * (1.0 / 240))))
    return y * jnp.exp(-(shift + tail) - offset)


def digamma(x):
    return jnp.log(exp_digamma(x, 0.0))


def expected_theta(gamma):
    return exp_digamma(gamma, digamma(jnp.sum(gamma, 1, keepdims=True))).astype(jnp.bfloat16)


def dense_counts(counts, place, rows, words):
    slots, tile, _ = counts.shape
    across = words // tile
    at = place[:, 0] * across + place[:, 1]
    slot_of = jnp.sum(jnp.where(at[:, None] == jnp.arange(slots)[None, :], jnp.arange(slots)[:, None], 0), 0)
    tiles = jnp.take(counts, slot_of, axis=0).astype(jnp.float32)
    return tiles.reshape(rows // tile, across, tile, tile).transpose(0, 2, 1, 3).reshape(rows, words)


def on_device(lambda_topics, gamma_start, tile_counts, tile_place, tile_live):
    rows, words = gamma_start.shape[0], lambda_topics.shape[1]
    counts = dense_counts(tile_counts[0, 0], tile_place[0, 0], rows, words)
    rowsum = lax.psum(jnp.sum(lambda_topics, 1), "vocab")
    share_beta = exp_digamma(lambda_topics, digamma(rowsum)[:, None]).astype(jnp.bfloat16)
    exp_beta = lax.all_gather(share_beta, "docs", axis=0, tiled=True)
    exp_theta = expected_theta(gamma_start)
    own_rows = rows // lax.axis_size("vocab")
    own_start = lax.axis_index("vocab") * own_rows

    def ratio_of(exp_theta):
        norm = jnp.dot(exp_theta, exp_beta, preferred_element_type=jnp.float32)
        return jnp.where(counts > 0, counts / norm, 0.0).astype(jnp.bfloat16)

    for step in range(3):
        part = lax.dot_general(
            ratio_of(exp_theta), exp_beta, (((1,), (1,)), ((), ())), preferred_element_type=jnp.float32
        )
        total = lax.psum_scatter(part.astype(jnp.bfloat16), "vocab", scatter_dimension=0, tiled=True)
        own_theta = lax.dynamic_slice_in_dim(exp_theta, own_start, own_rows, 0)
        gamma = alpha_prior + own_theta.astype(jnp.float32) * total.astype(jnp.float32)
        exp_theta = lax.all_gather(expected_theta(gamma), "vocab", axis=0, tiled=True)
    part_g = lax.dot_general(
        exp_theta, ratio_of(exp_theta), (((0,), (0,)), ((), ())), preferred_element_type=jnp.float32
    )
    sstats = lax.psum_scatter(part_g.astype(jnp.bfloat16), "docs", scatter_dimension=0, tiled=True)
    lambda_new = (1.0 - step_weight) * lambda_topics + step_weight * (
        eta_prior + corpus_scale * share_beta.astype(jnp.float32) * sstats.astype(jnp.float32)
    )
    return (gamma, lambda_new)


def solution(mesh):
    return jax.shard_map(
        on_device,
        mesh=mesh,
        in_specs=(
            P("docs", "vocab"),
            P(("parts", "docs"), None),
            P(("parts", "docs"), "vocab", None, None, None),
            P(("parts", "docs"), "vocab", None, None),
            P(("parts", "docs"), "vocab"),
        ),
        out_specs=(P(("parts", "docs", "vocab"), None), P(("parts", "docs"), "vocab")),
        check_vma=False,
    )
```

time: 749 us -> 318 us (0.42)
  loops' own time: 158 us -> 0 us
  matrix products: 151 us -> 30 us
  other arithmetic: 142 us -> 29.1 us
  local copies, waits for them, and re-layouts: 57.4 us -> 2.47 us
  waiting for transfers between devices: 213 us -> 232 us
    another operation x5 -> x0, loops' own time: 158 us -> none  [the longest x4 126 us: tile_pass(): return lax.fori_loop(0, live, tile_one_tile, (ratios, total))]
    psum x3 -> x0, waiting for transfers between devices: 152 us -> none  [on_device(): lax.psum(partial_value.astype(jnp.bfloat16), 'vocab').astype(jnp.float32)]
    dot_general x80 -> x4, matrix products: 151 us -> 30 us  [the longest x3 22.5 us: on_device(): lax.dot_general(ratio_of(exp_theta), exp_beta, (((1,), (1,)), ((), ())),...]
    all_gather x0 -> x3, waiting for transfers between devices: none -> 85.2 us  [on_device(): lax.all_gather(expected_theta(gamma), 'vocab', axis=0, tiled=True)]
    convert_element_type x9 -> x6, other arithmetic: 101 us -> 16.6 us  [the longest x4 10.2 us: expected_theta(): exp_digamma(gamma, digamma(jnp.sum(gamma, 1, keepdims=True)))]
    reduce_scatter x1 -> x4, waiting for transfers between devices: 40.6 us -> 119 us  [the longest x3 75.7 us: on_device(): lax.psum_scatter(part.astype(jnp.bfloat16), 'vocab', scatter_dimension=0,...]
    dynamic_slice x81 -> x0, local copies, waits for them, and re-layouts: 52.1 us -> none  [the longest x48 29.8 us: tile_one_tile(): col_start = place[position, 1] * TILE]
    reduce_sum x4 -> x5, other arithmetic: 21.6 us -> 5.51 us  [the longest x4 5.42 us: expected_theta(): jnp.sum(gamma, 1, keepdims=True)]
  transfers between devices with their start and end apart: 5 -> 8, of which waited for: 5 -> 8; matrix products, arithmetic and copies ran while one was open for 3% -> 3% of each run, Pallas kernels for 0% -> 0%
where the time goes in v1:
time: 318 us; the launch traced here: 315 us
  waiting for transfers between devices  232 us (73%)
  matrix products  30 us (9%)
  other arithmetic  29.1 us (9%)
  between operations  14.3 us (4%)
  blocking collectives  7.26 us (2%)
    all_gather x3, waiting for transfers between devices, on_device(): lax.all_gather(expected_theta(gamma), 'vocab', axis=0, tiled=True)  85.2 us
    reduce_scatter x3, waiting for transfers between devices, on_device(): lax.psum_scatter(part.astype(jnp.bfloat16), 'vocab', scatter_dimension=0,...  75.7 us
    reduce_scatter x1, waiting for transfers between devices, on_device(): lax.psum_scatter(part_g.astype(jnp.bfloat16), 'docs', scatter_dimension=0...  43.5 us
    all_gather x1, waiting for transfers between devices, on_device(): exp_beta = lax.all_gather(share_beta, 'docs', axis=0, tiled=True)  27.1 us
    dot_general x3, matrix products, on_device(): lax.dot_general(ratio_of(exp_theta), exp_beta, (((1,), (1,)), ((), ())),...  22.5 us
    convert_element_type x4, other arithmetic, expected_theta(): exp_digamma(gamma, digamma(jnp.sum(gamma, 1, keepdims=True)))  10.2 us
    dot_general x1, matrix products, on_device(): lax.dot_general(exp_theta, ratio_of(exp_theta), (((0,), (0,)), ((), ())),...  7.48 us
    psum x1, blocking collectives, on_device(): rowsum = lax.psum(jnp.sum(lambda_topics, 1), 'vocab')  7.26 us
  transfers between devices with their start and end apart: 8, of which 8 were waited for; matrix products, arithmetic and copies ran while one was open for 3% of the time, Pallas kernels for 0%

profile of v1, /device:TPU:11, one launch (start us, length us, event | category | flops | bytes accessed | tf_op | source)
XLA Modules:
  0.0 315.2 jit_solution(13760661573722015904)
XLA Ops:
  7.2 0.0 copy-start
  7.2 0.0 all-gather.5.cloned.1.call-start
  7.2 1.9 reduce_sum.62
  9.2 7.3 %psum.7 = f32[512]{0:T(512)S(1)} all-reduce(f32[512]{0:T(512)S(1)} %reduce_sum.62), channel_id=1, replica_groups=mesh['parts'=2,'vocab'=4,'docs'=4] {'vocab'}, use_global_device_ids=true, to_apply=%region_3.4 | all-reduce | flops 512 | bytes 4096 | tf_op jit(solution)/shard_map/psum | solution.py:44
  16.5 0.0 copy-start.4
  16.5 3.3 %multiply_convert_fusion = bf16[512,1024]{1,0:T(8,128)(2,1)} fusion(f32[512,1024]{1,0:T(8,128)S(1)} %copy-done.1, f32[512]{0:T(512)S(1)} %multiply_log_fusion), kind=kLoop, calls=%fused_computation.10 | loop fusion | flops 15728640 | bytes 3147776 | tf_op jit(solution)/shard_map/convert_element_type | solution.py:45
  19.8 0.0 all-gather.5.cloned.1.call-update
  19.8 0.0 reduce-scatter.5.cloned.1.call-start
  19.9 0.1 select_reduce_fusion
  19.9 0.1 reduce_sum.60
  20.0 1.8 reduce_sum.58
  21.8 1.6 gather_fusion
  23.5 3.1 fusion.9
  26.6 3.1 multiply_convert_fusion.1
  29.7 27.1 %all-gather.5.cloned.1.call-done = bf16[2048,1024]{1,0:T(8,128)(2,1)} async-done(((bf16[512,1024]{1,0:T(8,128)(2,1)}), bf16[2048,1024]{1,0:T(8,128)(2,1)}) %all-gather.5.cloned.1.call-update) | async-done | bytes 4194320 | tf_op jit(solution)/shard_map/all_gather | solution.py:46
  56.8 7.5 %convolution_convert_fusion.3 = bf16[256,2048]{1,0:T(8,128)(2,1)} fusion(bf16[2048,1024]{1,0:T(8,128)(2,1)} %all-gather.5.cloned.1.call-done, bf16[256,2048]{1,0:T(8,128)(2,1)} %multiply_convert_fusion.1, f32[32,8,8,128]{3,2,1,0:T(8,128)} %bitcast.56), kind=kOutput, calls=%fused_computation.8 | convolution fusion | flops 2149056512 | bytes 7340032 | tf_op jit(solution)/shard_map/dot_general | solution.py:56
  64.3 0.0 reduce-scatter.5.cloned.1.call-update
  64.3 0.0 all-gather.7.cloned.1.call-start
  64.4 25.7 %reduce-scatter.5.cloned.1.call-done = bf16[64,2048]{1,0:T(8,128)(2,1)} async-done(((bf16[256,2048]{1,0:T(8,128)(2,1)}), bf16[64,2048]{1,0:T(8,128)(2,1)}) %reduce-scatter.5.cloned.1.call-update) | async-done | bytes 262160 | tf_op jit(solution)/shard_map/reduce_scatter | solution.py:59
  90.1 1.2 add_reduce_fusion.1
  91.3 2.4 multiply_convert_fusion.4
  93.7 0.0 all-gather.7.cloned.1.call-update
  93.7 0.0 reduce-scatter.7.cloned.1.call-start
  93.8 28.4 %all-gather.7.cloned.1.call-done = bf16[256,2048]{1,0:T(8,128)(2,1)} async-done(((bf16[64,2048]{1,0:T(8,128)(2,1)}), bf16[256,2048]{1,0:T(8,128)(2,1)}) %all-gather.7.cloned.1.call-update) | async-done | bytes 1048592 | tf_op jit(solution)/shard_map/all_gather | solution.py:62
  122.2 7.5 %convolution_convert_fusion.2 = bf16[256,2048]{1,0:T(8,128)(2,1)} fusion(bf16[2048,1024]{1,0:T(8,128)(2,1)} %all-gather.5.cloned.1.call-done, bf16[256,2048]{1,0:T(8,128)(2,1)} %all-gather.7.cloned.1.call-done, f32[32,8,8,128]{3,2,1,0:T(8,128)} %bitcast.57), kind=kOutput, calls=%fused_computation.7 | convolution fusion | flops 2149056512 | bytes 7340032 | tf_op jit(solution)/shard_map/dot_general | solution.py:56
  129.7 0.0 reduce-scatter.7.cloned.1.call-update
  129.8 0.0 all-gather.9.cloned.1.call-start
  129.8 25.0 %reduce-scatter.7.cloned.1.call-done = bf16[64,2048]{1,0:T(8,128)(2,1)} async-done(((bf16[256,2048]{1,0:T(8,128)(2,1)}), bf16[64,2048]{1,0:T(8,128)(2,1)}) %reduce-scatter.7.cloned.1.call-update) | async-done | bytes 262160 | tf_op jit(solution)/shard_map/reduce_scatter | solution.py:59
  154.8 1.2 add_reduce_fusion
  156.1 2.4 multiply_convert_fusion.3
  158.4 0.0 all-gather.9.cloned.1.call-update
  158.4 0.2 reduce-scatter.9.cloned.1.call-start
  158.7 28.3 %all-gather.9.cloned.1.call-done = bf16[256,2048]{1,0:T(8,128)(2,1)} async-done(((bf16[64,2048]{1,0:T(8,128)(2,1)}), bf16[256,2048]{1,0:T(8,128)(2,1)}) %all-gather.9.cloned.1.call-update) | async-done | bytes 1048592 | tf_op jit(solution)/shard_map/all_gather | solution.py:62
  187.0 7.5 %convolution_convert_fusion.1 = bf16[256,2048]{1,0:T(8,128)(2,1)} fusion(bf16[2048,1024]{1,0:T(8,128)(2,1)} %all-gather.5.cloned.1.call-done, bf16[256,2048]{1,0:T(8,128)(2,1)} %all-gather.9.cloned.1.call-done, f32[32,8,8,128]{3,2,1,0:T(8,128)} %bitcast.58), kind=kOutput, calls=%fused_computation.6 | convolution fusion | flops 2149056512 | bytes 7340032 | tf_op jit(solution)/shard_map/dot_general | solution.py:56
  194.5 0.0 reduce-scatter.9.cloned.1.call-update
  194.5 0.0 all-gather.11.cloned.1.call-start
  194.5 25.0 %reduce-scatter.9.cloned.1.call-done = bf16[64,2048]{1,0:T(8,128)(2,1)} async-done(((bf16[256,2048]{1,0:T(8,128)(2,1)}), bf16[64,2048]{1,0:T(8,128)(2,1)}) %reduce-scatter.9.cloned.1.call-update) | async-done | bytes 262160 | tf_op jit(solution)/shard_map/reduce_scatter | solution.py:59
  219.5 1.2 fusion.21
  220.7 0.0 copy-start.3
  220.8 0.8 copy-done.3
  221.5 2.3 multiply_convert_fusion.2
  223.9 0.0 all-gather.11.cloned.1.call-update
  223.9 0.0 reduce-scatter.11.cloned.1.call-start
  224.0 28.5 %all-gather.11.cloned.1.call-done = bf16[256,2048]{1,0:T(8,128)(2,1)} async-done(((bf16[64,2048]{1,0:T(8,128)(2,1)}), bf16[256,2048]{1,0:T(8,128)(2,1)}) %all-gather.11.cloned.1.call-update) | async-done | bytes 1048592 | tf_op jit(solution)/shard_map/all_gather | solution.py:62
  252.4 7.5 %convolution_convert_fusion = bf16[2048,1024]{1,0:T(8,128)(2,1)} fusion(bf16[256,2048]{1,0:T(8,128)(2,1)} %all-gather.11.cloned.1.call-done, bf16[2048,1024]{1,0:T(8,128)(2,1)} %all-gather.5.cloned.1.call-done, f32[32,8,8,128]{3,2,1,0:T(8,128)} %bitcast.59), kind=kOutput, calls=%fused_computation.1 | convolution fusion | flops 2150629376 | bytes 10485760 | tf_op jit(solution)/shard_map/dot_general | solution.py:63
  259.9 0.0 reduce-scatter.11.cloned.1.call-update
  259.9 43.5 %reduce-scatter.11.cloned.1.call-done = bf16[512,1024]{1,0:T(8,128)(2,1)} async-done(((bf16[2048,1024]{1,0:T(8,128)(2,1)}), bf16[512,1024]{1,0:T(8,128)(2,1)}) %reduce-scatter.11.cloned.1.call-update) | async-done | bytes 1048592 | tf_op jit(solution)/shard_map/reduce_scatter | solution.py:66
  303.4 5.0 %add_multiply_fusion.4 = f32[512,1024]{1,0:T(8,128)} fusion(f32[512,1024]{1,0:T(8,128)S(1)} %copy-done.1, bf16[512,1024]{1,0:T(8,128)(2,1)} %reduce-scatter.11.cloned.1.call-done, f32[512]{0:T(512)S(1)} %multiply_log_fusion), kind=kLoop, calls=%fused_computation.9 | loop fusion | flops 19398656 | bytes 5244928 | tf_op jit(solution)/shard_map/add | solution.py:67
  (15 shorter events, 0.2 us)
Async XLA Ops:
  7.2 14.7 %copy-start = (s32[1,1,16,128,128]{4,3,2,1,0:T(8,128)S(1)}, s32[1,1,16,128,128]{4,3,2,1,0:T(8,128)}, u32[]{:S(2)}) copy-start(s32[1,1,16,128,128]{4,3,2,1,0:T(8,128)} %param.7) | copy-start | bytes 3145732
  7.2 9.3 %copy-start.1 = (f32[512,1024]{1,0:T(8,128)S(1)}, f32[512,1024]{1,0:T(8,128)}, u32[]{:S(2)}) copy-start(f32[512,1024]{1,0:T(8,128)} %param.5) | copy-start | bytes 6291460
  7.2 49.6 %all-gather.5.cloned.1.call-start = ((), (), s32[]{:S(2)}) async-start(), calls=%async_computation.4 | async-start | bytes 5242880 | tf_op jit(solution)/shard_map/all_gather | solution.py:46
  16.5 3.4 %copy-start.4 = (s32[1,1,16,2]{2,3,1,0:T(2,128)S(1)}, s32[1,1,16,2]{2,3,1,0:T(2,128)}, u32[]{:S(2)}) copy-start(s32[1,1,16,2]{2,3,1,0:T(2,128)} %param.8) | copy-start | bytes 388
  19.8 70.3 %reduce-scatter.5.cloned.1.call-start = ((), (), s32[]{:S(2)}) async-start(), calls=%async_computation.5 | async-start | bytes 1310720 | tf_op jit(solution)/shard_map/reduce_scatter | solution.py:59
  23.4 3.1 copy-start.2
  64.3 57.9 %all-gather.7.cloned.1.call-start = ((), (), s32[]{:S(2)}) async-start(), calls=%async_computation.6 | async-start | bytes 1310720 | tf_op jit(solution)/shard_map/all_gather | solution.py:62
  93.7 61.1 %reduce-scatter.7.cloned.1.call-start = ((), (), s32[]{:S(2)}) async-start(), calls=%async_computation.7 | async-start | bytes 1310720 | tf_op jit(solution)/shard_map/reduce_scatter | solution.py:59
  129.8 57.2 %all-gather.9.cloned.1.call-start = ((), (), s32[]{:S(2)}) async-start(), calls=%async_computation.8 | async-start | bytes 1310720 | tf_op jit(solution)/shard_map/all_gather | solution.py:62
  158.4 61.1 %reduce-scatter.9.cloned.1.call-start = ((), (), s32[]{:S(2)}) async-start(), calls=%async_computation.9 | async-start | bytes 1310720 | tf_op jit(solution)/shard_map/reduce_scatter | solution.py:59
  194.5 57.9 %all-gather.11.cloned.1.call-start = ((), (), s32[]{:S(2)}) async-start(), calls=%async_computation.10 | async-start | bytes 1310720 | tf_op jit(solution)/shard_map/all_gather | solution.py:62
  220.7 0.8 copy-start.3
  223.9 79.5 %reduce-scatter.11.cloned.1.call-start = ((), (), s32[]{:S(2)}) async-start(), calls=%async_computation.11 | async-start | bytes 5242880 | tf_op jit(solution)/shard_map/reduce_scatter | solution.py:66
Sparse Core Ops, SparseCore 0:
  19.9 36.8 all-gather.4
  64.4 25.6 reduce-scatter.4
  93.9 28.3 all-gather.6
  129.9 24.8 reduce-scatter.6
  158.6 28.3 all-gather.8
  194.6 24.8 reduce-scatter.8
  224.0 28.3 all-gather.10
  260.0 43.3 reduce-scatter.10

commit v2 on v1

v2 whole, which is shorter than its diff:
```python
import functools

import jax
import jax.numpy as jnp
from jax import lax
from jax.experimental import pallas as pl
from jax.experimental.pallas import tpu as pltpu
from jax.sharding import PartitionSpec as P

MESH = pl.DeviceIdType.MESH
ITERS = 3
UNIT = 32
TILE = 128
CHUNKS = 4
alpha_prior = 0.05
eta_prior = 0.01
step_weight = 0.5
corpus_scale = 4.0


def exp_digamma(x, offset):
    y = x + 4.0
    a = x * (x + 3.0)
    p = a * (a + 2.0)
    r = 1.0 / (p * y)
    q = p * r
    s = q * q
    shift = (2.0 * x + 3.0) * (2.0 * a + 2.0) * (y * r)
    tail = q * 0.5 + s * (1.0 / 12 - s * (1.0 / 120 - s * (1.0 / 252 - s * (1.0 / 240))))
    return y * jnp.exp(-(shift + tail) - offset)


def digamma(x):
    return jnp.log(exp_digamma(x, 0.0))


def remote(src, dst, send, recv, **where):
    return pltpu.make_async_remote_copy(
        src_ref=src, dst_ref=dst, send_sem=send, recv_sem=recv, device_id=where, device_id_type=MESH
    )


def kernel(
    nv, nd, place_ref, lam_ref, gamma_ref, counts_ref, gamma_out, lam_out,
    sums, shift, cd, beta, theta, part, ratio, from_left, from_right, to_right, to_left, gam, thall, rall, acc,
    sum_send, sum_recv, beta_send, beta_recv, rs, rr, ls, lr, th_send, th_recv, ra_send, ra_recv, fw_send,
):
    p, v, d = lax.axis_index("parts"), lax.axis_index("vocab"), lax.axis_index("docs")
    core = lax.rem(d, 2)
    sib = d + 1 - 2 * core
    share, words = lam_ref.shape
    rows, topics = gamma_ref.shape
    nb = 4
    block = rows // nb
    units = block // UNIT
    nx = nd // 2
    chip = lax.div(d, 2)
    others = [lax.rem(chip + i, nx) * 2 + core for i in range(1, nx)]
    peers = [lax.rem(d + i, nd) for i in range(1, nd)]

    barrier = pltpu.get_barrier_semaphore()
    for i in range(1, nv):
        pl.semaphore_signal(barrier, inc=1, device_id={"vocab": lax.rem(v + i, nv)}, device_id_type=MESH)
    for peer in peers:
        pl.semaphore_signal(barrier, inc=1, device_id={"docs": peer}, device_id_type=MESH)
    pl.semaphore_signal(barrier, inc=1, device_id={"parts": 1 - p}, device_id_type=MESH)

    folded = lam_ref[:, 0:TILE]
    for i in range(1, words // TILE):
        folded = folded + lam_ref[:, i * TILE : (i + 1) * TILE]
    sums[v] = jnp.broadcast_to(jnp.sum(folded.T, 0, keepdims=True), (8, share))
    pl.semaphore_wait(barrier, nv - 1 + nd - 1 + 1)

    def sum_copy(i):
        return remote(sums.at[v], sums.at[v], sum_send.at[i], sum_recv.at[v], vocab=lax.rem(v + i, nv))

    for i in range(1, nv):
        sum_copy(i).start()

    def first_theta(i, carry):
        at = pl.ds(pl.multiple_of(i * 16, 16), 16)
        g = gamma_ref[at, :]
        theta[at, :] = exp_digamma(g, digamma(jnp.sum(g, 1, keepdims=True))).astype(jnp.bfloat16)
        return carry

    lax.fori_loop(0, rows // 16, first_theta, 0)

    for i in range(1, nv):
        src = lax.rem(v + nv - i, nv)
        remote(sums.at[src], sums.at[src], sum_send.at[i], sum_recv.at[src], vocab=src).wait_recv()
    whole = sums[0]
    for i in range(1, nv):
        whole = whole + sums[i]
    shift[...] = jnp.broadcast_to(digamma(whole)[0:1], (TILE, share)).T

    piece = share // (2 * CHUNKS)

    def region(owner, c):
        return beta.at[pl.ds(pl.multiple_of(owner * share + c * piece, piece), piece)]

    def beta_copy(owner, c, slot, **where):
        return remote(region(owner, c), region(owner, c), beta_send.at[slot], beta_recv.at[owner, c], **where)

    sends = []

    def send_beta(owner, c, **where):
        copy = beta_copy(owner, c, len(sends), **where)
        copy.start()
        sends.append(copy)

    for j in range(2 * CHUNKS):
        c = lax.rem(p * CHUNKS + j, 2 * CHUNKS)

        def own_beta(i, carry, c=c):
            at = pl.ds(pl.multiple_of(c * piece + i * 16, 16), 16)
            to = pl.ds(pl.multiple_of(d * share + c * piece + i * 16, 16), 16)
            off = jnp.concatenate([shift[at, :]] * (words // TILE), 1)
            beta[to, :] = exp_digamma(lam_ref[at, :], off).astype(jnp.bfloat16)
            return carry

        lax.fori_loop(0, piece // 16, own_beta, 0)
        if j < CHUNKS:
            for other in others:
                send_beta(d, c, docs=other)
        send_beta(d, c, docs=sib)

    slots = counts_ref.shape[0]
    across = words // TILE
    for r in range(rows // TILE):
        for k in range(across):
            slot = jnp.int32(0)
            for s in range(slots):
                hit = place_ref[s, 0] * across + place_ref[s, 1] == r * across + k
                slot = jnp.where(hit, s, slot)
            cd[r * TILE : (r + 1) * TILE, k * TILE : (k + 1) * TILE] = counts_ref[slot].astype(jnp.float32)

    @pl.when(v == 0)
    def _():
        from_left[...] = jnp.zeros_like(from_left)

    @pl.when(v == nv - 1)
    def _():
        from_right[...] = jnp.zeros_like(from_right)

    for j in range(CHUNKS):
        c = p * CHUNKS + j
        for other in others:
            beta_copy(other, c, 0, docs=other).wait_recv()
            send_beta(other, c, parts=1 - p)
            send_beta(other, c, docs=sib)
    for j in range(CHUNKS):
        c = (1 - p) * CHUNKS + j
        for other in others:
            beta_copy(other, c, 0, docs=other).wait_recv()
            send_beta(other, c, docs=sib)
    for c in range(2 * CHUNKS):
        beta_copy(sib, c, 0, docs=sib).wait_recv()
        for other in others:
            far = other + 1 - 2 * core
            beta_copy(far, c, 0, docs=sib).wait_recv()

    def unit_rows(t, u):
        return pl.ds(pl.multiple_of(lax.rem(t, nb) * block + u * UNIT, UNIT), UNIT)

    def right_copy(t, u):
        it, at, n = lax.div(t, nb), unit_rows(t, u), lax.rem(t, nb) * units + u
        return remote(to_right.at[it, at], from_left.at[it, at], rs.at[it, n], rr.at[it, n], vocab=lax.rem(v + 1, nv))

    def left_copy(t, u):
        it, at, n = lax.div(t, nb), unit_rows(t, u), lax.rem(t, nb) * units + u
        return remote(
            to_left.at[it, at], from_right.at[it, at], ls.at[it, n], lr.at[it, n], vocab=lax.rem(v + nv - 1, nv)
        )

    total_steps = ITERS * nb

    def pass_right(t):
        for u in range(units):
            it, at = lax.div(t, nb), unit_rows(t, u)

            @pl.when(v > 0)
            def _():
                right_copy(t, u).wait_recv()

            to_right[it, at, :] = (part[at, :] + from_left[it, at, :].astype(jnp.float32)).astype(jnp.bfloat16)
            right_copy(t, u).start()

    def pass_left(t):
        for u in range(units):
            it, at = lax.div(t, nb), unit_rows(t, u)

            @pl.when(v < nv - 1)
            def _():
                left_copy(t, u).wait_recv()

            to_left[it, at, :] = (part[at, :] + from_right[it, at, :].astype(jnp.float32)).astype(jnp.bfloat16)
            left_copy(t, u).start()

    def finish(t):
        it = lax.div(t, nb)
        for u in range(units):

            @pl.when(v == nv - 1)
            def _():
                right_copy(t, u).wait_recv()

            @pl.when(v == 0)
            def _():
                left_copy(t, u).wait_recv()

            def some(i, carry):
                at = pl.ds(pl.multiple_of(lax.rem(t, nb) * block + u * UNIT + i * 16, 16), 16)
                total = part[at, :] + (
                    from_left[it, at, :].astype(jnp.float32) + from_right[it, at, :].astype(jnp.float32)
                )
                g = alpha_prior + theta[at, :].astype(jnp.float32) * total
                gam[at, :] = g
                theta[at, :] = exp_digamma(g, digamma(jnp.sum(g, 1, keepdims=True))).astype(jnp.bfloat16)
                return carry

            lax.fori_loop(0, UNIT // 16, some, 0)

    def th_copy(b, to):
        at = pl.ds(pl.multiple_of(b * block, block), block)
        cols = pl.ds(pl.multiple_of(to * share, share), share)
        return remote(theta.at[at, cols], thall.at[b, d], th_send.at[b, to], th_recv.at[b, d], docs=to)

    def ra_copy(b, to):
        at = pl.ds(pl.multiple_of(b * block, block), block)
        return remote(ratio.at[at], rall.at[b, d], ra_send.at[b, to], ra_recv.at[b, d], docs=to)

    def fw_copy(b, owner):
        return remote(rall.at[b, owner], rall.at[b, owner], fw_send.at[b, owner], ra_recv.at[b, owner], docs=sib)

    def th_from(b, owner):
        return remote(thall.at[b, owner], thall.at[b, owner], th_send.at[b, owner], th_recv.at[b, owner], docs=sib)

    wide = 256

    def compute(s):
        b = lax.rem(s, nb)
        at = pl.ds(pl.multiple_of(b * block, block), block)
        th = theta[at, :]
        for k in range(words // wide):
            cols = slice(k * wide, (k + 1) * wide)
            norm = jnp.dot(th, beta[:, cols], preferred_element_type=jnp.float32)
            c = cd[at, cols]
            ratio[at, cols] = jnp.where(c > 0.0, c / norm, 0.0).astype(jnp.bfloat16)

        @pl.when(s < total_steps)
        def _():
            ra = ratio[at, :]
            for k in range(topics // wide):
                cols = slice(k * wide, (k + 1) * wide)
                part[at, cols] = lax.dot_general(
                    ra, beta[cols, :], (((1,), (1,)), ((), ())), preferred_element_type=jnp.float32
                )

        @pl.when(s >= total_steps)
        def _():
            for other in others:
                ra_copy(b, other).start()
            for to in peers:
                th_copy(b, to).start()
            ra_copy(b, sib).start()
            thall[b, d] = theta[at, pl.ds(pl.multiple_of(d * share, share), share)]
            rall[b, d] = ratio[at, :]

    def forward(b):
        for other in others:
            fw_copy(b, other).wait_recv()
            fw_copy(b, other).start()

    def collect(b):
        for peer in peers:
            th_from(b, peer).wait_recv()
        fw_copy(b, sib).wait_recv()
        for other in others:
            fw_copy(b, other + 1 - 2 * core).wait_recv()
        left = thall[b].reshape(nd * block, share)
        for k in range(words // wide):
            cols = slice(k * wide, (k + 1) * wide)
            right = rall[b, :, :, cols].reshape(nd * block, wide)
            more = lax.dot_general(left, right, (((0,), (0,)), ((), ())), preferred_element_type=jnp.float32)
            acc[:, cols] = acc[:, cols] + more

    acc[...] = jnp.zeros_like(acc)
    lag_right = jnp.minimum(v, 2)
    lag_left = jnp.minimum(nv - 1 - v, 2)

    def step(s, carry):
        t_right = s - lag_right

        @pl.when((v > 0) & (v < nv - 1) & (t_right >= 0) & (t_right < total_steps))
        def _():
            pass_right(t_right)

        t_left = s - lag_left

        @pl.when((v > 0) & (v < nv - 1) & (t_left >= 0) & (t_left < total_steps))
        def _():
            pass_left(t_left)

        @pl.when(s < total_steps + nb)
        def _():
            compute(s)

        @pl.when((v == 0) & (s < total_steps))
        def _():
            pass_right(s)

        @pl.when((v == nv - 1) & (s < total_steps))
        def _():
            pass_left(s)

        @pl.when((s >= 3) & (s < total_steps + 3))
        def _():
            finish(s - 3)

        @pl.when(s > total_steps)
        def _():
            @pl.when(s <= total_steps + nb)
            def _():
                forward(s - total_steps - 1)

            @pl.when(s > total_steps + 1)
            def _():
                collect(s - total_steps - 2)

        return carry

    lax.fori_loop(0, total_steps + nb + 2, step, 0)

    own = gamma_out.shape[0]
    gamma_out[...] = gam[pl.ds(pl.multiple_of(v * own, own), own), :]

    def update(i, carry):
        at = pl.ds(pl.multiple_of(i * 16, 16), 16)
        mine = beta[pl.ds(pl.multiple_of(d * share + i * 16, 16), 16), :].astype(jnp.float32)
        lam_out[at, :] = (1.0 - step_weight) * lam_ref[at, :] + step_weight * (
            eta_prior + corpus_scale * mine * acc[at, :]
        )
        return carry

    lax.fori_loop(0, share // 16, update, 0)

    for i in range(1, nv):
        sum_copy(i).wait_send()
    for copy in sends:
        copy.wait_send()

    def drain(t, carry):
        for u in range(units):

            @pl.when(v < nv - 1)
            def _():
                right_copy(t, u).wait_send()

            @pl.when(v > 0)
            def _():
                left_copy(t, u).wait_send()

        return carry

    lax.fori_loop(0, total_steps, drain, 0)

    def drain_last(b, carry):
        for other in others:
            ra_copy(b, other).wait_send()
            fw_copy(b, other).wait_send()
        ra_copy(b, sib).wait_send()
        for to in peers:
            th_copy(b, to).wait_send()
        return carry

    lax.fori_loop(0, nb, drain_last, 0)


def on_device(nv, nd, lambda_topics, gamma_start, tile_counts, tile_place, tile_live):
    share, words = lambda_topics.shape
    rows, topics = gamma_start.shape
    nb, nx = 4, nd // 2
    nsend = CHUNKS * (2 + (nx - 1) * 4)
    vmem = pl.BlockSpec(memory_space=pltpu.VMEM)
    bf, f32 = jnp.bfloat16, jnp.float32
    dma = pltpu.SemaphoreType.DMA
    units = rows // UNIT
    moving = pltpu.VMEM((ITERS, rows, topics), bf)
    return pl.pallas_call(
        functools.partial(kernel, nv, nd),
        out_shape=(
            jax.ShapeDtypeStruct((rows // nv, topics), f32),
            jax.ShapeDtypeStruct((share, words), f32),
        ),
        in_specs=[pl.BlockSpec(memory_space=pltpu.SMEM), vmem, vmem, vmem],
        out_specs=(vmem, vmem),
        scratch_shapes=[
            pltpu.VMEM((nv, 8, share), f32),
            pltpu.VMEM((share, TILE), f32),
            pltpu.VMEM((rows, words), f32),
            pltpu.VMEM((topics, words), bf),
            pltpu.VMEM((rows, topics), bf),
            pltpu.VMEM((rows, topics), f32),
            pltpu.VMEM((rows, words), bf),
            moving, moving, moving, moving,
            pltpu.VMEM((rows, topics), f32),
            pltpu.VMEM((nb, nd, rows // nb, share), bf),
            pltpu.VMEM((nb, nd, rows // nb, words), bf),
            pltpu.VMEM((share, words), f32),
            dma((nv,)), dma((nv,)),
            dma((nsend,)), dma((nd, 2 * CHUNKS)),
            dma((ITERS, units)), dma((ITERS, units)), dma((ITERS, units)), dma((ITERS, units)),
            dma((nb, nd)), dma((nb, nd)), dma((nb, nd)), dma((nb, nd)), dma((nb, nd)),
        ],
        compiler_params=pltpu.CompilerParams(
            collective_id=0, has_side_effects=True, vmem_limit_bytes=56 * 1024 * 1024
        ),
    )(tile_place[0, 0], lambda_topics, gamma_start, tile_counts[0, 0])


def solution(mesh):
    return jax.shard_map(
        functools.partial(on_device, mesh.shape["vocab"], mesh.shape["docs"]),
        mesh=mesh,
        in_specs=(
            P("docs", "vocab"),
            P(("parts", "docs"), None),
            P(("parts", "docs"), "vocab", None, None, None),
            P(("parts", "docs"), "vocab", None, None),
            P(("parts", "docs"), "vocab"),
        ),
        out_specs=(P(("parts", "docs", "vocab"), None), P(("parts", "docs"), "vocab")),
        check_vma=False,
    )
```

time: 318 us -> 139 us (0.44)
  waiting for transfers between devices: 232 us -> 0 us
  Pallas kernels: 0 us -> 132 us
  matrix products: 30 us -> 0 us
  other arithmetic: 29.1 us -> 0 us
  between operations: 14.3 us -> 0.64 us
  blocking collectives: 7.26 us -> 0 us
  local copies, waits for them, and re-layouts: 2.47 us -> 6.38 us
    pallas_call x0 -> x1, Pallas kernels: none -> 132 us  [on_device(): pl.pallas_call(functools.partial(kernel, nv, nd), out_shape=(jax.ShapeDty...]
    reduce_scatter x4 -> x0, waiting for transfers between devices: 119 us -> none  [the longest x3 75.7 us: on_device(): lax.psum_scatter(part.astype(jnp.bfloat16), 'vocab', scatter_dimension=0,...]
    all_gather x4 -> x0, waiting for transfers between devices: 112 us -> none  [the longest x3 85.2 us: on_device(): lax.all_gather(expected_theta(gamma), 'vocab', axis=0, tiled=True)]
    dot_general x4 -> x0, matrix products: 30 us -> none  [the longest x3 22.5 us: on_device(): lax.dot_general(ratio_of(exp_theta), exp_beta, (((1,), (1,)), ((), ())),...]
    convert_element_type x6 -> x0, other arithmetic: 16.6 us -> none  [the longest x4 10.2 us: expected_theta(): exp_digamma(gamma, digamma(jnp.sum(gamma, 1, keepdims=True)))]
    reduce_sum x6 -> x0, other arithmetic: 7.42 us -> none  [the longest x4 5.42 us: expected_theta(): jnp.sum(gamma, 1, keepdims=True)]
    psum x1 -> x0, blocking collectives: 7.26 us -> none  [on_device(): rowsum = lax.psum(jnp.sum(lambda_topics, 1), 'vocab')]
    add x1 -> x0, other arithmetic: 4.95 us -> none  [on_device(): (1.0 - step_weight) * lambda_topics]
  transfers between devices with their start and end apart: 8 -> 0, of which waited for: 8 -> 0; matrix products, arithmetic and copies ran while one was open for 3% -> 0% of each run, Pallas kernels for 0% -> 0%
where the time goes in v2:
time: 139 us
  Pallas kernels  132 us (95%)
  local copies, waits for them, and re-layouts  6.38 us (5%)
    pallas_call x1, Pallas kernels, on_device(): pl.pallas_call(functools.partial(kernel, nv, nd), out_shape=(jax.ShapeDty...  132 us
    unnamed x2, local copies, waits for them, and re-layouts  5.03 us

profile of v2, /device:TPU:11, one launch (start us, length us, event | category | flops | bytes accessed | tf_op | source)
XLA Modules:
  0.0 139.2 jit_solution(7023332846453070346)
XLA Ops:
  0.6 1.4 copy.6.place_ref
  2.0 132.2 %shard_map.59 = (f32[64,2048]{1,0:T(8,128)}, f32[512,1024]{1,0:T(8,128)}) custom-call(s32[16,2]{1,0:T(8,128)} %copy.6.place_ref, f32[512,1024]{1,0:T(8,128)} %lam_ref.1, f32[256,2048]{1,0:T(8,128)} %gamma_ref.1, s32[16,128,128]{2,1,0:T(8,128)} %bitcast.2), custom_call_target="tpu_custom_call" | custom-call | tf_op jit(solution)/shard_map/pallas_call | solution.py:389
  134.2 1.9 %copy.9 = f32[64,2048]{1,0:T(8,128)} copy(f32[64,2048]{1,0:T(8,128)} %get-tuple-element.4) | data formatting | bytes 1048576
  136.1 3.2 %copy.10 = f32[512,1024]{1,0:T(8,128)} copy(f32[512,1024]{1,0:T(8,128)} %get-tuple-element.5) | data formatting | bytes 4194304

commit v3 on v2

--- a/solution.py
+++ b/solution.py
@@ -9,9 +9,9 @@
 
 MESH = pl.DeviceIdType.MESH
 ITERS = 3
-UNIT = 32
+UNIT = 16
 TILE = 128
-CHUNKS = 4
+CHUNKS = 8
 alpha_prior = 0.05
 eta_prior = 0.01
 step_weight = 0.5
@@ -41,11 +41,17 @@
 
 
 def kernel(
-    nv, nd, place_ref, lam_ref, gamma_ref, counts_ref, gamma_out, lam_out,
-    sums, shift, cd, beta, theta, part, ratio, from_left, from_right, to_right, to_left, gam, thall, rall, acc,
-    sum_send, sum_recv, beta_send, beta_recv, rs, rr, ls, lr, th_send, th_recv, ra_send, ra_recv, fw_send,
+    nv, nd, place_ref, lam_hbm, gamma_hbm, counts_hbm, gamma_out, lam_out,
+    lam_ref, gamma_ref, counts_ref, lam_new, load_sem, store_sem, sums, offs, off, psums, cd, beta, theta, part, ratio, from_left, from_right, to_right, to_left, gam, thall, rall, acc,
+    sum_send, sum_recv, off_send, off_recv, beta_send, beta_recv, rs, rr, ls, lr, th_send, th_recv, ra_send, ra_recv, fw_send,
 ):
     p, v, d = lax.axis_index("parts"), lax.axis_index("vocab"), lax.axis_index("docs")
+    load_lam = pltpu.make_async_copy(lam_hbm, lam_ref, load_sem.at[0])
+    load_gamma = pltpu.make_async_copy(gamma_hbm, gamma_ref, load_sem.at[1])
+    load_counts = pltpu.make_async_copy(counts_hbm, counts_ref, load_sem.at[2])
+    load_lam.start()
+    load_counts.start()
+    load_gamma.start()
     core = lax.rem(d, 2)
     sib = d + 1 - 2 * core
     share, words = lam_ref.shape
@@ -65,11 +71,39 @@
         pl.semaphore_signal(barrier, inc=1, device_id={"docs": peer}, device_id_type=MESH)
     pl.semaphore_signal(barrier, inc=1, device_id={"parts": 1 - p}, device_id_type=MESH)
 
+    piece = share // (2 * CHUNKS)
+
+    def region(owner, c):
+        return beta.at[pl.ds(pl.multiple_of(owner * share + c * piece, piece), piece)]
+
+    def beta_copy(owner, c, slot, **where):
+        return remote(region(owner, c), region(owner, c), beta_send.at[slot], beta_recv.at[owner, c], **where)
+
+    sends = []
+
+    def send_beta(owner, c, **where):
+        copy = beta_copy(owner, c, len(sends), **where)
+        copy.start()
+        sends.append(copy)
+
+    load_lam.wait()
+    for j in range(2 * CHUNKS):
+        c = lax.rem(p * CHUNKS + j, 2 * CHUNKS)
+        for i in range(piece // 16):
+            at = pl.ds(pl.multiple_of(c * piece + i * 16, 16), 16)
+            to = pl.ds(pl.multiple_of(d * share + c * piece + i * 16, 16), 16)
+            beta[to, :] = exp_digamma(lam_ref[at, :], 0.0).astype(jnp.bfloat16)
+        if j == 0:
+            pl.semaphore_wait(barrier, nv - 1 + nd - 1 + 1)
+        if j < CHUNKS:
+            for other in others:
+                send_beta(d, c, docs=other)
+        send_beta(d, c, docs=sib)
+
     folded = lam_ref[:, 0:TILE]
     for i in range(1, words // TILE):
         folded = folded + lam_ref[:, i * TILE : (i + 1) * TILE]
     sums[v] = jnp.broadcast_to(jnp.sum(folded.T, 0, keepdims=True), (8, share))
-    pl.semaphore_wait(barrier, nv - 1 + nd - 1 + 1)
 
     def sum_copy(i):
         return remote(sums.at[v], sums.at[v], sum_send.at[i], sum_recv.at[v], vocab=lax.rem(v + i, nv))
@@ -77,60 +111,14 @@
     for i in range(1, nv):
         sum_copy(i).start()
 
-    def first_theta(i, carry):
-        at = pl.ds(pl.multiple_of(i * 16, 16), 16)
-        g = gamma_ref[at, :]
-        theta[at, :] = exp_digamma(g, digamma(jnp.sum(g, 1, keepdims=True))).astype(jnp.bfloat16)
-        return carry
-
-    lax.fori_loop(0, rows // 16, first_theta, 0)
-
-    for i in range(1, nv):
-        src = lax.rem(v + nv - i, nv)
-        remote(sums.at[src], sums.at[src], sum_send.at[i], sum_recv.at[src], vocab=src).wait_recv()
-    whole = sums[0]
-    for i in range(1, nv):
-        whole = whole + sums[i]
-    shift[...] = jnp.broadcast_to(digamma(whole)[0:1], (TILE, share)).T
-
-    piece = share // (2 * CHUNKS)
-
-    def region(owner, c):
-        return beta.at[pl.ds(pl.multiple_of(owner * share + c * piece, piece), piece)]
-
-    def beta_copy(owner, c, slot, **where):
-        return remote(region(owner, c), region(owner, c), beta_send.at[slot], beta_recv.at[owner, c], **where)
-
-    sends = []
-
-    def send_beta(owner, c, **where):
-        copy = beta_copy(owner, c, len(sends), **where)
-        copy.start()
-        sends.append(copy)
-
-    for j in range(2 * CHUNKS):
-        c = lax.rem(p * CHUNKS + j, 2 * CHUNKS)
-
-        def own_beta(i, carry, c=c):
-            at = pl.ds(pl.multiple_of(c * piece + i * 16, 16), 16)
-            to = pl.ds(pl.multiple_of(d * share + c * piece + i * 16, 16), 16)
-            off = jnp.concatenate([shift[at, :]] * (words // TILE), 1)
-            beta[to, :] = exp_digamma(lam_ref[at, :], off).astype(jnp.bfloat16)
-            return carry
-
-        lax.fori_loop(0, piece // 16, own_beta, 0)
-        if j < CHUNKS:
-            for other in others:
-                send_beta(d, c, docs=other)
-        send_beta(d, c, docs=sib)
-
     slots = counts_ref.shape[0]
     across = words // TILE
+    load_counts.wait()
     for r in range(rows // TILE):
         for k in range(across):
             slot = jnp.int32(0)
             for s in range(slots):
-                hit = place_ref[s, 0] * across + place_ref[s, 1] == r * across + k
+                hit = place_ref[0, s] * across + place_ref[1, s] == r * across + k
                 slot = jnp.where(hit, s, slot)
             cd[r * TILE : (r + 1) * TILE, k * TILE : (k + 1) * TILE] = counts_ref[slot].astype(jnp.float32)
 
@@ -142,17 +130,67 @@
     def _():
         from_right[...] = jnp.zeros_like(from_right)
 
+    acc[...] = jnp.zeros_like(acc)
+
+    def off_copy(i):
+        return remote(offs.at[d], offs.at[d], off_send.at[i], off_recv.at[d], docs=lax.rem(d + i, nd))
+
+    def send_offs():
+        for i in range(1, nv):
+            src = lax.rem(v + nv - i, nv)
+            remote(sums.at[src], sums.at[src], sum_send.at[i], sum_recv.at[src], vocab=src).wait_recv()
+        whole = sums[0]
+        for i in range(1, nv):
+            whole = whole + sums[i]
+        offs[d] = digamma(whole)
+        for i in range(1, nd):
+            off_copy(i).start()
+
+    def take_offs():
+        for i in range(1, nd):
+            src = lax.rem(d + nd - i, nd)
+            remote(offs.at[src], offs.at[src], off_send.at[i], off_recv.at[src], docs=src).wait_recv()
+        for i in range(nd):
+            off[:, i * share : (i + 1) * share] = offs[i]
+        load_gamma.wait()
+
+    def set_theta(at, n):
+        for i in range(n // 16):
+            part_of = pl.ds(pl.multiple_of(at + i * 16, 16), 16)
+            psums[i * 16 : (i + 1) * 16, :] = jnp.broadcast_to(jnp.sum(gam[part_of, :], 1, keepdims=True), (16, TILE))
+        psums[0:n, :] = digamma(psums[0:n, :])
+        for i in range(n // 16):
+            part_of = pl.ds(pl.multiple_of(at + i * 16, 16), 16)
+            offset = psums[i * 16 : (i + 1) * 16, 0:1] + off[0:1, :]
+            theta[part_of, :] = exp_digamma(gam[part_of, :], offset).astype(jnp.bfloat16)
+
+    first = rows // 8
+
+    def first_theta(i):
+        at = pl.ds(i * first, first)
+        gam[at, :] = gamma_ref[at, :]
+        set_theta(i * first, first)
+
     for j in range(CHUNKS):
         c = p * CHUNKS + j
         for other in others:
             beta_copy(other, c, 0, docs=other).wait_recv()
             send_beta(other, c, parts=1 - p)
             send_beta(other, c, docs=sib)
+        if j == 1:
+            send_offs()
+        if j == CHUNKS - 3:
+            take_offs()
+        if j >= CHUNKS - 3:
+            first_theta(j - CHUNKS + 3)
     for j in range(CHUNKS):
         c = (1 - p) * CHUNKS + j
         for other in others:
             beta_copy(other, c, 0, docs=other).wait_recv()
             send_beta(other, c, docs=sib)
+        if j % 2 == 0:
+            first_theta(3 + j // 2)
+    first_theta(7)
     for c in range(2 * CHUNKS):
         beta_copy(sib, c, 0, docs=sib).wait_recv()
         for other in others:
@@ -208,17 +246,17 @@
             def _():
                 left_copy(t, u).wait_recv()
 
-            def some(i, carry):
-                at = pl.ds(pl.multiple_of(lax.rem(t, nb) * block + u * UNIT + i * 16, 16), 16)
-                total = part[at, :] + (
-                    from_left[it, at, :].astype(jnp.float32) + from_right[it, at, :].astype(jnp.float32)
-                )
-                g = alpha_prior + theta[at, :].astype(jnp.float32) * total
-                gam[at, :] = g
-                theta[at, :] = exp_digamma(g, digamma(jnp.sum(g, 1, keepdims=True))).astype(jnp.bfloat16)
-                return carry
-
-            lax.fori_loop(0, UNIT // 16, some, 0)
+            at = unit_rows(t, u)
+            total = part[at, :] + (
+                from_left[it, at, :].astype(jnp.float32) + from_right[it, at, :].astype(jnp.float32)
+            )
+            gam[at, :] = alpha_prior + theta[at, :].astype(jnp.float32) * total
+        set_theta(lax.rem(t, nb) * block, block)
+
+        @pl.when(t >= total_steps - nb)
+        def _():
+            for to in peers:
+                th_copy(lax.rem(t, nb), to).start()
 
     def th_copy(b, to):
         at = pl.ds(pl.multiple_of(b * block, block), block)
@@ -260,8 +298,6 @@
         def _():
             for other in others:
                 ra_copy(b, other).start()
-            for to in peers:
-                th_copy(b, to).start()
             ra_copy(b, sib).start()
             thall[b, d] = theta[at, pl.ds(pl.multiple_of(d * share, share), share)]
             rall[b, d] = ratio[at, :]
@@ -284,10 +320,13 @@
             more = lax.dot_general(left, right, (((0,), (0,)), ((), ())), preferred_element_type=jnp.float32)
             acc[:, cols] = acc[:, cols] + more
 
-    acc[...] = jnp.zeros_like(acc)
     lag_right = jnp.minimum(v, 2)
     lag_left = jnp.minimum(nv - 1 - v, 2)
 
+    own = gamma_out.shape[0]
+    own_at = pl.ds(pl.multiple_of(v * own, own), own)
+    store_gamma = pltpu.make_async_copy(gam.at[own_at], gamma_out, store_sem.at[0])
+
     def step(s, carry):
         t_right = s - lag_right
 
@@ -317,6 +356,10 @@
         def _():
             finish(s - 3)
 
+        @pl.when(s == total_steps + 3)
+        def _():
+            store_gamma.start()
+
         @pl.when(s > total_steps)
         def _():
             @pl.when(s <= total_steps + nb)
@@ -331,19 +374,26 @@
 
     lax.fori_loop(0, total_steps + nb + 2, step, 0)
 
-    own = gamma_out.shape[0]
-    gamma_out[...] = gam[pl.ds(pl.multiple_of(v * own, own), own), :]
-
-    def update(i, carry):
-        at = pl.ds(pl.multiple_of(i * 16, 16), 16)
-        mine = beta[pl.ds(pl.multiple_of(d * share + i * 16, 16), 16), :].astype(jnp.float32)
-        lam_out[at, :] = (1.0 - step_weight) * lam_ref[at, :] + step_weight * (
-            eta_prior + corpus_scale * mine * acc[at, :]
-        )
-        return carry
-
-    lax.fori_loop(0, share // 16, update, 0)
-
+    big = share // 4
+    stores = []
+    for k in range(4):
+
+        def update(i, carry, k=k):
+            at = pl.ds(pl.multiple_of(k * big + i * 16, 16), 16)
+            mine = beta[pl.ds(pl.multiple_of(d * share + k * big + i * 16, 16), 16), :].astype(jnp.float32)
+            lam_new[at, :] = (1.0 - step_weight) * lam_ref[at, :] + step_weight * (
+                eta_prior + corpus_scale * mine * acc[at, :]
+            )
+            return carry
+
+        lax.fori_loop(0, big // 16, update, 0)
+        at = pl.ds(k * big, big)
+        store = pltpu.make_async_copy(lam_new.at[at], lam_out.at[at], store_sem.at[1 + k])
+        store.start()
+        stores.append(store)
+
+    for i in range(1, nd):
+        off_copy(i).wait_send()
     for i in range(1, nv):
         sum_copy(i).wait_send()
     for copy in sends:
@@ -374,6 +424,9 @@
         return carry
 
     lax.fori_loop(0, nb, drain_last, 0)
+    for store in stores:
+        store.wait()
+    store_gamma.wait()
 
 
 def on_device(nv, nd, lambda_topics, gamma_start, tile_counts, tile_place, tile_live):
@@ -381,7 +434,7 @@
     rows, topics = gamma_start.shape
     nb, nx = 4, nd // 2
     nsend = CHUNKS * (2 + (nx - 1) * 4)
-    vmem = pl.BlockSpec(memory_space=pltpu.VMEM)
+    hbm = pl.BlockSpec(memory_space=pl.ANY)
     bf, f32 = jnp.bfloat16, jnp.float32
     dma = pltpu.SemaphoreType.DMA
     units = rows // UNIT
@@ -392,11 +445,18 @@
             jax.ShapeDtypeStruct((rows // nv, topics), f32),
             jax.ShapeDtypeStruct((share, words), f32),
         ),
-        in_specs=[pl.BlockSpec(memory_space=pltpu.SMEM), vmem, vmem, vmem],
-        out_specs=(vmem, vmem),
+        in_specs=[pl.BlockSpec(memory_space=pltpu.SMEM), hbm, hbm, hbm],
+        out_specs=(hbm, hbm),
         scratch_shapes=[
+            pltpu.VMEM((share, words), f32),
+            pltpu.VMEM((rows, topics), f32),
+            pltpu.VMEM(tile_counts.shape[2:], jnp.int32),
+            pltpu.VMEM((share, words), f32),
+            dma((3,)), dma((5,)),
             pltpu.VMEM((nv, 8, share), f32),
-            pltpu.VMEM((share, TILE), f32),
+            pltpu.VMEM((nd, 8, share), f32),
+            pltpu.VMEM((8, topics), f32),
+            pltpu.VMEM((rows // nb, TILE), f32),
             pltpu.VMEM((rows, words), f32),
             pltpu.VMEM((topics, words), bf),
             pltpu.VMEM((rows, topics), bf),
@@ -407,7 +467,7 @@
             pltpu.VMEM((nb, nd, rows // nb, share), bf),
             pltpu.VMEM((nb, nd, rows // nb, words), bf),
             pltpu.VMEM((share, words), f32),
-            dma((nv,)), dma((nv,)),
+            dma((nv,)), dma((nv,)), dma((nd,)), dma((nd,)),
             dma((nsend,)), dma((nd, 2 * CHUNKS)),
             dma((ITERS, units)), dma((ITERS, units)), dma((ITERS, units)), dma((ITERS, units)),
             dma((nb, nd)), dma((nb, nd)), dma((nb, nd)), dma((nb, nd)), dma((nb, nd)),
@@ -415,7 +475,7 @@
         compiler_params=pltpu.CompilerParams(
             collective_id=0, has_side_effects=True, vmem_limit_bytes=56 * 1024 * 1024
         ),
-    )(tile_place[0, 0], lambda_topics, gamma_start, tile_counts[0, 0])
+    )(tile_place[0, 0].T, lambda_topics, gamma_start, tile_counts[0, 0])
 
 
 def solution(mesh):

time: 139 us -> 133 us (0.957)
  Pallas kernels: 132 us -> 127 us
    pallas_call x1, Pallas kernels: 132 us -> 127 us  [on_device(): pl.pallas_call(functools.partial(kernel, nv, nd), out_shape=(jax.ShapeDty...]
where the time goes in v3:
time: 133 us
  Pallas kernels  127 us (95%)
  local copies, waits for them, and re-layouts  5.03 us (4%)
    pallas_call x1, Pallas kernels, on_device(): pl.pallas_call(functools.partial(kernel, nv, nd), out_shape=(jax.ShapeDty...  127 us
    unnamed x2, local copies, waits for them, and re-layouts  5.03 us

profile of v3, /device:TPU:11, one launch (start us, length us, event | category | flops | bytes accessed | tf_op | source)
XLA Modules:
  0.0 132.5 jit_solution(12395508714750912896)
XLA Ops:
  0.6 126.9 %shard_map.59 = (f32[64,2048]{1,0:T(8,128)}, f32[512,1024]{1,0:T(8,128)}) custom-call(s32[2,16]{1,0:T(2,128)} %bitcast.5, f32[512,1024]{1,0:T(8,128)} %lam_hbm.1, f32[256,2048]{1,0:T(8,128)} %gamma_hbm.1, s32[16,128,128]{2,1,0:T(8,128)} %bitcast.4), custom_call_target="tpu_custom_call" | custom-call | tf_op jit(solution)/shard_map/pallas_call | solution.py:442
  127.5 1.9 %copy.8 = f32[64,2048]{1,0:T(8,128)} copy(f32[64,2048]{1,0:T(8,128)} %get-tuple-element.4) | data formatting | bytes 1048576
  129.4 3.2 %copy.9 = f32[512,1024]{1,0:T(8,128)} copy(f32[512,1024]{1,0:T(8,128)} %get-tuple-element.5) | data formatting | bytes 4194304
